TPU v7x, 128 devices: a whole 4x4x4 slice. The times are simulated.
128 devices in a mesh: wa: 32 (over y, z, core), row: 4 (over x).
Axes of the slice: x: 4, y: 4, z: 4, core: 2. Of those that a mesh axis runs over, the one named last changes fastest.
Arguments:
- rhs: float32 [4096, 128], P(('wa', 'row')), may hold values from -6 to 6
- tiles0: float32 [4096, 5, 128, 128], P(('wa', 'row')), may hold values from -0.25 to 0.25
- diag0: float32 [4096, 128], P(('wa', 'row')), may hold values from 1.5 to 4.5
- cols0: int32 [4096, 4], P(('wa', 'row')), may hold values from 0 to 4095, as said below
- tiles1: float32 [1024, 5, 128, 128], P(('wa', 'row')), may hold values from -0.25 to 0.25
- diag1: float32 [1024, 128], P(('wa', 'row')), may hold values from 1.5 to 4.5
- cols1: int32 [1024, 4], P(('wa', 'row')), may hold values from 0 to 1023, as said below
- tiles2: float32 [16, 5, 128, 128], replicated, may hold values from -0.25 to 0.25
- diag2: float32 [16, 128], replicated, may hold values from 1.5 to 4.5
- cols2: int32 [16, 4], replicated, may hold values from 0 to 15
- interp0: float32 [4096, 128, 128], P(('wa', 'row')), may hold values from -0.5 to 0.5
- owner0: int32 [4096], P(('wa', 'row')), may hold values from 0 to 1023, as said below
- interp1: float32 [1024, 128, 128], P(('wa', 'row')), may hold values from -0.5 to 0.5
- owner1: int32 [1024], P(('wa', 'row')), may hold values from 0 to 15
Outputs:
- solution: float32 [4096, 128], P(('wa', 'row'))
- coarse_correction: float32 [1024, 128], P('wa')
- coarsest_correction: float32 [16, 128], replicated
Inputs may be any that keep to these rules, and one draw needn't show every extreme that they name: cols0[i, k] lies within 32 of i; cols0[i, 0] lies exactly 32 away from i, on a side drawn per row, unless that leaves the level, where it is clipped to the level's end. cols1[j, k] lies within 32 of j; cols1[j, 0] lies exactly 32 away from j, on a side drawn per row, unless that leaves the level, where it is clipped to the level's end. owner0[i] lies between 32 * (i // 128) and that plus 32 - 1.
All inputs are finite; a program needn't handle non-finite values.
Results may differ from a plain program's by a relative error of at most 0.00021.
Values sent between devices are 32-bit elements; how exact they have to be, the bound alone decides.
A program may use at most 128 MiB of HBM per device.

v0:
```python
import jax
import jax.numpy as jnp
from jax import lax
from jax.sharding import PartitionSpec as P

SWEEPS = 2


relax = 0.8
highest = lax.Precision.HIGHEST


def with_halo(value, sides, width):
    for axis, dim in sides:
        size, length = (lax.axis_size(axis), value.shape[dim])
        up = [(i, (i + 1) % size) for i in range(size - 1)]
        down = [(j, i) for i, j in up]
        last = lax.slice_in_dim(value, length - width, length, axis=dim)
        leading = lax.slice_in_dim(value, 0, width, axis=dim)
        before = lax.ppermute(last, axis, up)
        after = lax.ppermute(leading, axis, down)
        value = jnp.concatenate([before, value, after], axis=dim)
    return value


def inverse_diagonal(tiles, diag):
    return 1.0 / (diag + jnp.einsum("bii->bi", tiles[:, 0]))


def tile_product(tiles, diag, own, picked):
    stacked = jnp.concatenate([own[:, None, :], picked], axis=1)
    return diag * own + jnp.einsum("bkij,bkj->bi", tiles, stacked, precision=highest)


def fine_apply(tiles0, diag0, local0, field):
    extended = with_halo(field, ((("wa", "row"), 0),), field.shape[0])
    return tile_product(tiles0, diag0, field, extended[local0])


def coarse_rim(full):
    return with_halo(full, (("wa", 0),), full.shape[0])


def shards(
    rhs,
    tiles0,
    diag0,
    cols0,
    tiles1,
    diag1,
    cols1,
    tiles2,
    diag2,
    cols2,
    interp0,
    owner0,
    interp1,
    owner1,
):
    rows0 = rhs.shape[0]
    group = lax.axis_index("wa")
    local0 = cols0 - lax.axis_index(("wa", "row")) * rows0 + rows0
    slots = jnp.arange(rows0, dtype=jnp.int32)
    marks = jnp.arange(tiles2.shape[0], dtype=jnp.int32)
    inv0 = inverse_diagonal(tiles0, diag0)
    field0 = relax * rhs * inv0
    field0 = field0 + relax * (rhs - fine_apply(tiles0, diag0, local0, field0)) * inv0
    resid0 = rhs - fine_apply(tiles0, diag0, local0, field0)
    lifted0 = jnp.einsum("bij,bi->bj", interp0, resid0, precision=highest)
    match0 = (owner0[:, None] - group * rows0 == slots[None, :]).astype(jnp.float32)
    term1 = jnp.dot(match0.T, lifted0, precision=highest)
    inv2 = inverse_diagonal(tiles2, diag2)
    right1 = lax.psum(term1, "row")
    tiles_g, diag_g, cols_g, interp_g, owner_g = (
        lax.all_gather(tiles1, "row", axis=0, tiled=True),
        lax.all_gather(diag1, "row", axis=0, tiled=True),
        lax.all_gather(cols1, "row", axis=0, tiled=True),
        lax.all_gather(interp1, "row", axis=0, tiled=True),
        lax.all_gather(owner1, "row", axis=0, tiled=True),
    )
    local1 = cols_g - group * rows0 + rows0
    inv1 = inverse_diagonal(tiles_g, diag_g)

    def coarse_apply(field):
        return tile_product(tiles_g, diag_g, field, coarse_rim(field)[local1])

    field1 = relax * right1 * inv1
    field1 = field1 + relax * (right1 - coarse_apply(field1)) * inv1
    resid1 = right1 - coarse_apply(field1)
    match1 = (owner_g[:, None] == marks[None, :]).astype(jnp.float32)
    lifted1 = jnp.einsum("bij,bi->bj", interp_g, resid1, precision=highest)
    term2 = jnp.dot(match1.T, lifted1, precision=highest)
    right2 = lax.psum(term2, "wa")
    field2 = relax * right2 * inv2
    field2 = field2 + relax * (right2 - tile_product(tiles2, diag2, field2, field2[cols2])) * inv2
    picked2 = jnp.dot(match1, field2, precision=highest)
    field1 = field1 + jnp.einsum("bij,bj->bi", interp_g, picked2, precision=highest)
    for sweep in range(SWEEPS):
        field1 = field1 + relax * (right1 - coarse_apply(field1)) * inv1
    picked1 = jnp.dot(match0, field1, precision=highest)
    field0 = field0 + jnp.einsum("bij,bj->bi", interp0, picked1, precision=highest)
    for sweep in range(SWEEPS):
        field0 = field0 + relax * (rhs - fine_apply(tiles0, diag0, local0, field0)) * inv0
    return (field0, field1, field2)


def solution(mesh):
    in_specs = (
        P(("wa", "row"), None),
        P(("wa", "row"), None, None, None),
        P(("wa", "row"), None),
        P(("wa", "row"), None),
        P(("wa", "row"), None, None, None),
        P(("wa", "row"), None),
        P(("wa", "row"), None),
        P(),
        P(),
        P(),
        P(("wa", "row"), None, None),
        P(("wa", "row")),
        P(("wa", "row"), None, None),
        P(("wa", "row")),
    )
    out_specs = (P(("wa", "row"), None), P("wa", None), P())
    return jax.shard_map(shards, mesh=mesh, in_specs=in_specs, out_specs=out_specs, check_vma=False)
```

profile of v0, /device:TPU:8, one launch (start us, length us, event | category | flops | bytes accessed | tf_op | source)
XLA Modules:
  0.0 422.2 jit_solution(4974700073033468074)
XLA Ops:
  9.6 11.2 %all-gather = s32[4,8,4]{1,2,0:T(4,128)S(1)} all-gather(s32[1,8,4]{1,2,0:T(4,128)} %bitcast.179), channel_id=1, replica_groups=mesh['wa'=32,'row'=4] {'row'}, dimensions={0}, use_global_device_ids=true | all-gather | bytes 640 | tf_op jit(solution)/shard_map/all_gather | solution.py:77
  22.4 90.5 %all-gather.4.cloned.1.call-done = f32[32,5,128,128]{3,2,1,0:T(8,128)} async-done(((f32[8,5,128,128]{3,2,1,0:T(8,128)}), f32[32,5,128,128]{3,2,1,0:T(8,128)}) %all-gather.4.cloned.1.call-update) | async-done | bytes 10485776 | tf_op jit(solution)/shard_map/all_gather | solution.py:75
  119.8 6.4 %collective-permute-start.1 = (f32[32,128]{1,0:T(8,128)S(1)}, f32[32,128]{1,0:T(8,128)S(1)}, u32[]{:S(2)}, u32[]{:S(2)}) collective-permute-start(f32[32,128]{1,0:T(8,128)S(1)} %multiply_multiply_fusion.1), channel_id=1, source_target_pairs={{1,0},{2,1},{3,2},{4,3},{5,4},{6,5},{7,6},{8,7},{9,8},{10,9},{11,1... | collective-permute-start | bytes 49160 | tf_op jit(solution)/shard_map/ppermute | solution.py:21
  128.3 12.6 %fusion.18 = f32[32,1,128,1]{2,1,3,0:T(1,128)S(1)} fusion(f32[32,5,128,128]{3,2,1,0:T(8,128)} %param.15, f32[32,5,128,1]{2,1,0,3:T(8,128)S(1)} %maximum_bitcast_fusion), kind=kOutput, calls=%fused_computation.38 | convolution fusion | flops 31457280 | bytes 10584064 | tf_op jit(solution)/shard_map/bkij,bkj->bi/dot_general | solution.py:32
  143.0 7.9 %collective-permute-start.3 = (f32[32,128]{1,0:T(8,128)S(1)}, f32[32,128]{1,0:T(8,128)S(1)}, u32[]{:S(2)}, u32[]{:S(2)}) collective-permute-start(f32[32,128]{1,0:T(8,128)S(1)} %multiply_add_fusion.5), channel_id=1, source_target_pairs={{1,0},{2,1},{3,2},{4,3},{5,4},{6,5},{7,6},{8,7},{9,8},{10,9},{11,1... | collective-permute-start | bytes 49160 | tf_op jit(solution)/shard_map/ppermute | solution.py:21
  152.4 12.1 %all_gather.15 = f32[32,128]{1,0:T(8,128)S(1)} all-gather(f32[8,128]{1,0:T(8,128)S(1)} %copy-done.6), channel_id=1, replica_groups=mesh['wa'=32,'row'=4] {'row'}, dimensions={0}, use_global_device_ids=true | all-gather | bytes 20480 | tf_op jit(solution)/shard_map/all_gather | solution.py:76
  165.3 12.6 %fusion.16 = f32[32,1,128,1]{2,1,3,0:T(1,128)S(1)} fusion(f32[32,5,128,128]{3,2,1,0:T(8,128)} %param.15, f32[32,5,128,1]{2,1,0,3:T(8,128)S(1)} %maximum_bitcast_fusion.1), kind=kOutput, calls=%fused_computation.36 | convolution fusion | flops 31457280 | bytes 10584064 | tf_op jit(solution)/shard_map/bkij,bkj->bi/dot_general | solution.py:32
  180.1 14.3 %psum.14 = f32[32,128]{1,0:T(8,128)S(1)} all-reduce(f32[32,128]{1,0:T(8,128)S(1)} %fusion.25), channel_id=1, replica_groups=mesh['wa'=32,'row'=4] {'row'}, use_global_device_ids=true, to_apply=%region_1.0 | all-reduce | flops 4096 | bytes 32768 | tf_op jit(solution)/shard_map/psum | solution.py:73
  196.3 5.8 %collective-permute-start.5 = (f32[32,128]{1,0:T(8,128)S(1)}, f32[32,128]{1,0:T(8,128)S(1)}, u32[]{:S(2)}, u32[]{:S(2)}) collective-permute-start(f32[32,128]{1,0:T(8,128)S(1)} %multiply_multiply_fusion), channel_id=1, source_target_pairs={{4,0},{8,4},{12,8},{16,12},{20,16},{24,20},{28,24},{32,28},{36,32}... | collective-permute-start | bytes 49160 | tf_op jit(solution)/shard_map/ppermute | solution.py:21
  204.2 12.6 %fusion.14 = f32[32,1,128,1]{2,1,3,0:T(1,128)S(1)} fusion(f32[32,5,128,128]{3,2,1,0:T(8,128)} %all-gather.4.cloned.1.call-done, f32[32,5,128,1]{2,1,0,3:T(8,128)S(1)} %maximum_bitcast_fusion.2), kind=kOutput, calls=%fused_computation.34 | convolution fusion | flops 31457280 | bytes 10584064 | tf_op jit(solution)/shard_map/bkij,bkj->bi/dot_general | solution.py:32
  218.8 5.8 %collective-permute-start.7 = (f32[32,128]{1,0:T(8,128)S(1)}, f32[32,128]{1,0:T(8,128)S(1)}, u32[]{:S(2)}, u32[]{:S(2)}) collective-permute-start(f32[32,128]{1,0:T(8,128)S(1)} %multiply_add_fusion.4), channel_id=1, source_target_pairs={{4,0},{8,4},{12,8},{16,12},{20,16},{24,20},{28,24},{32,28},{36,32}... | collective-permute-start | bytes 49160 | tf_op jit(solution)/shard_map/ppermute | solution.py:21
  226.1 6.9 %all-reduce = s32[32]{0:T(128)S(1)} all-reduce(s32[32]{0:T(128)S(1)} %dynamic-update-slice), channel_id=1, replica_groups=mesh['wa'=32,'row'=4] {'row'}, use_global_device_ids=true, to_apply=%add | all-reduce | flops 32 | bytes 256
  233.7 12.6 %fusion.12 = f32[32,1,128,1]{2,1,3,0:T(1,128)S(1)} fusion(f32[32,5,128,128]{3,2,1,0:T(8,128)} %all-gather.4.cloned.1.call-done, f32[32,5,128,1]{2,1,0,3:T(8,128)S(1)} %maximum_bitcast_fusion.3), kind=kOutput, calls=%fused_computation.32 | convolution fusion | flops 31457280 | bytes 10584064 | tf_op jit(solution)/shard_map/bkij,bkj->bi/dot_general | solution.py:32
  250.1 54.0 %psum.15 = f32[16,128]{1,0:T(8,128)S(1)} all-reduce(f32[16,128]{1,0:T(8,128)S(1)} %fusion.23), channel_id=1, replica_groups=mesh['wa'=32,'row'=4] {'wa'}, use_global_device_ids=true, to_apply=%region_3.0 | all-reduce | flops 2048 | bytes 16384 | tf_op jit(solution)/shard_map/psum | solution.py:93
  304.7 7.0 %fusion.20 = f32[16,1,128,1]{2,1,3,0:T(1,128)S(1)} fusion(f32[16,5,128,128]{3,2,1,0:T(8,128)} %param.21, f32[16,5,128,1]{2,1,0,3:T(8,128)S(1)} %maximum_bitcast_fusion.8), kind=kOutput, calls=%fused_computation.50 | convolution fusion | flops 15728640 | bytes 5292032 | tf_op jit(solution)/shard_map/bkij,bkj->bi/dot_general | solution.py:32
  311.9 4.9 %fusion.32 = f32[32,1,128]{2,1,0:T(1,128)S(1)} fusion(f32[32,128,1]{1,2,0:T(1,128)S(1)} %bitcast.175, f32[32,128,128]{2,1,0:T(8,128)} %all-gather.6.cloned.1.call-done), kind=kOutput, calls=%fused_computation.88 | convolution fusion | flops 6291456 | bytes 2129920 | tf_op jit(solution)/shard_map/bij,bj->bi/dot_general | solution.py:97
  318.8 6.2 %collective-permute-start.9 = (f32[32,128]{1,0:T(8,128)S(1)}, f32[32,128]{1,0:T(8,128)S(1)}, u32[]{:S(2)}, u32[]{:S(2)}) collective-permute-start(f32[32,128]{1,0:T(8,128)S(1)} %add.119), channel_id=1, source_target_pairs={{4,0},{8,4},{12,8},{16,12},{20,16},{24,20},{28,24},{32,28},{36,32}... | collective-permute-start | bytes 49160 | tf_op jit(solution)/shard_map/ppermute | solution.py:21
  326.7 12.6 %fusion.10 = f32[32,1,128,1]{2,1,3,0:T(1,128)S(1)} fusion(f32[32,5,128,128]{3,2,1,0:T(8,128)} %all-gather.4.cloned.1.call-done, f32[32,5,128,1]{2,1,0,3:T(8,128)S(1)} %maximum_bitcast_fusion.4), kind=kOutput, calls=%fused_computation.30 | convolution fusion | flops 31457280 | bytes 10584064 | tf_op jit(solution)/shard_map/bkij,bkj->bi/dot_general | solution.py:32
  341.3 5.8 %collective-permute-start.11 = (f32[32,128]{1,0:T(8,128)S(1)}, f32[32,128]{1,0:T(8,128)S(1)}, u32[]{:S(2)}, u32[]{:S(2)}) collective-permute-start(f32[32,128]{1,0:T(8,128)S(1)} %multiply_add_fusion.3), channel_id=1, source_target_pairs={{4,0},{8,4},{12,8},{16,12},{20,16},{24,20},{28,24},{32,28},{36,32}... | collective-permute-start | bytes 49160 | tf_op jit(solution)/shard_map/ppermute | solution.py:21
  349.2 12.6 %fusion.8 = f32[32,1,128,1]{2,1,3,0:T(1,128)S(1)} fusion(f32[32,5,128,128]{3,2,1,0:T(8,128)} %all-gather.4.cloned.1.call-done, f32[32,5,128,1]{2,1,0,3:T(8,128)S(1)} %maximum_bitcast_fusion.5), kind=kOutput, calls=%fused_computation.28 | convolution fusion | flops 31457280 | bytes 10584064 | tf_op jit(solution)/shard_map/bkij,bkj->bi/dot_general | solution.py:32
  368.6 6.8 %collective-permute-start.13 = (f32[32,128]{1,0:T(8,128)S(1)}, f32[32,128]{1,0:T(8,128)S(1)}, u32[]{:S(2)}, u32[]{:S(2)}) collective-permute-start(f32[32,128]{1,0:T(8,128)S(1)} %add.124), channel_id=1, source_target_pairs={{1,0},{2,1},{3,2},{4,3},{5,4},{6,5},{7,6},{8,7},{9,8},{10,9},{11,1... | collective-permute-start | bytes 49160 | tf_op jit(solution)/shard_map/ppermute | solution.py:21
  377.3 12.6 %fusion.6 = f32[32,1,128,1]{2,1,3,0:T(1,128)S(1)} fusion(f32[32,5,128,128]{3,2,1,0:T(8,128)} %param.15, f32[32,5,128,1]{2,1,0,3:T(8,128)S(1)} %maximum_bitcast_fusion.6), kind=kOutput, calls=%fused_computation.26 | convolution fusion | flops 31457280 | bytes 10584064 | tf_op jit(solution)/shard_map/bkij,bkj->bi/dot_general | solution.py:32
  391.9 7.9 %collective-permute-start.15 = (f32[32,128]{1,0:T(8,128)S(1)}, f32[32,128]{1,0:T(8,128)S(1)}, u32[]{:S(2)}, u32[]{:S(2)}) collective-permute-start(f32[32,128]{1,0:T(8,128)S(1)} %multiply_add_fusion.1), channel_id=1, source_target_pairs={{1,0},{2,1},{3,2},{4,3},{5,4},{6,5},{7,6},{8,7},{9,8},{10,9},{11,1... | collective-permute-start | bytes 49160 | tf_op jit(solution)/shard_map/ppermute | solution.py:21
  401.9 12.6 %fusion.4 = f32[32,1,128,1]{2,1,3,0:T(1,128)S(1)} fusion(f32[32,5,128,128]{3,2,1,0:T(8,128)} %param.15, f32[32,5,128,1]{2,1,0,3:T(8,128)S(1)} %maximum_bitcast_fusion.7), kind=kOutput, calls=%fused_computation.24 | convolution fusion | flops 31457280 | bytes 10584064 | tf_op jit(solution)/shard_map/bkij,bkj->bi/dot_general | solution.py:32
  (118 shorter events, 52.3 us)
Async XLA Ops:
  7.2 170.8 %copy-start = (f32[32,128,128]{2,1,0:T(8,128)S(1)}, f32[32,128,128]{2,1,0:T(8,128)}, u32[]{:S(2)}) copy-start(f32[32,128,128]{2,1,0:T(8,128)} %param.24) | copy-start | bytes 6291460
  7.2 133.8 %copy-start.1 = (f32[32,128]{1,0:T(8,128)S(1)}, f32[32,128]{1,0:T(8,128)}, u32[]{:S(2)}) copy-start(f32[32,128]{1,0:T(8,128)} %param.14) | copy-start | bytes 49156
  7.2 133.8 %copy-start.2 = (f32[32,128]{1,0:T(8,128)S(1)}, f32[32,128]{1,0:T(8,128)}, u32[]{:S(2)}) copy-start(f32[32,128]{1,0:T(8,128)} %param.16) | copy-start | bytes 49156
  7.2 145.2 %copy-start.6 = (f32[8,128]{1,0:T(8,128)S(1)}, f32[8,128]{1,0:T(8,128)}, u32[]{:S(2)}) copy-start(f32[8,128]{1,0:T(8,128)} %param.19) | copy-start | bytes 12292
  7.2 105.7 %all-gather.4.cloned.1.call-start = ((), (), s32[]{:S(2)}) async-start(), calls=%async_computation | async-start | bytes 13107200 | tf_op jit(solution)/shard_map/all_gather | solution.py:75
  7.9 238.4 %all-gather.6.cloned.1.call-start = ((), (), s32[]{:S(2)}) async-start(), calls=%async_computation.1 | async-start | bytes 2621440 | tf_op jit(solution)/shard_map/all_gather | solution.py:78
  116.4 9.8 %collective-permute-start = (f32[32,128]{1,0:T(8,128)S(1)}, f32[32,128]{1,0:T(8,128)S(1)}, u32[]{:S(2)}, u32[]{:S(2)}) collective-permute-start(f32[32,128]{1,0:T(8,128)S(1)} %multiply_multiply_fusion.1), channel_id=1, source_target_pairs={{0,1},{1,2},{2,3},{3,4},{4,5},{5,6},{6,7},{7,8},{8,9},{9,10},{10,1... | collective-permute-start | bytes 49160 | tf_op jit(solution)/shard_map/ppermute | solution.py:20
  119.8 7.8 %collective-permute-start.1 = (f32[32,128]{1,0:T(8,128)S(1)}, f32[32,128]{1,0:T(8,128)S(1)}, u32[]{:S(2)}, u32[]{:S(2)}) collective-permute-start(f32[32,128]{1,0:T(8,128)S(1)} %multiply_multiply_fusion.1), channel_id=1, source_target_pairs={{1,0},{2,1},{3,2},{4,3},{5,4},{6,5},{7,6},{8,7},{9,8},{10,9},{11,1... | collective-permute-start | bytes 49160 | tf_op jit(solution)/shard_map/ppermute | solution.py:21
  141.0 23.5 %collective-permute-start.2 = (f32[32,128]{1,0:T(8,128)S(1)}, f32[32,128]{1,0:T(8,128)S(1)}, u32[]{:S(2)}, u32[]{:S(2)}) collective-permute-start(f32[32,128]{1,0:T(8,128)S(1)} %multiply_add_fusion.5), channel_id=1, source_target_pairs={{0,1},{1,2},{2,3},{3,4},{4,5},{5,6},{6,7},{7,8},{8,9},{9,10},{10,1... | collective-permute-start | bytes 49160 | tf_op jit(solution)/shard_map/ppermute | solution.py:20
  143.0 21.6 %collective-permute-start.3 = (f32[32,128]{1,0:T(8,128)S(1)}, f32[32,128]{1,0:T(8,128)S(1)}, u32[]{:S(2)}, u32[]{:S(2)}) collective-permute-start(f32[32,128]{1,0:T(8,128)S(1)} %multiply_add_fusion.5), channel_id=1, source_target_pairs={{1,0},{2,1},{3,2},{4,3},{5,4},{6,5},{7,6},{8,7},{9,8},{10,9},{11,1... | collective-permute-start | bytes 49160 | tf_op jit(solution)/shard_map/ppermute | solution.py:21
  165.2 60.6 %copy-start.7 = (s32[8]{0:T(128)S(1)}, s32[8]{0:T(128)}, u32[]{:S(2)}) copy-start(s32[8]{0:T(128)} %param.27) | copy-start | bytes 100
  194.4 7.9 %collective-permute-start.4 = (f32[32,128]{1,0:T(8,128)S(1)}, f32[32,128]{1,0:T(8,128)S(1)}, u32[]{:S(2)}, u32[]{:S(2)}) collective-permute-start(f32[32,128]{1,0:T(8,128)S(1)} %multiply_multiply_fusion), channel_id=1, source_target_pairs={{0,4},{4,8},{8,12},{12,16},{16,20},{20,24},{24,28},{28,32},{32,36}... | collective-permute-start | bytes 49160 | tf_op jit(solution)/shard_map/ppermute | solution.py:20
  196.3 7.2 %collective-permute-start.5 = (f32[32,128]{1,0:T(8,128)S(1)}, f32[32,128]{1,0:T(8,128)S(1)}, u32[]{:S(2)}, u32[]{:S(2)}) collective-permute-start(f32[32,128]{1,0:T(8,128)S(1)} %multiply_multiply_fusion), channel_id=1, source_target_pairs={{4,0},{8,4},{12,8},{16,12},{20,16},{24,20},{28,24},{32,28},{36,32}... | collective-permute-start | bytes 49160 | tf_op jit(solution)/shard_map/ppermute | solution.py:21
  204.1 99.9 %copy-start.3 = (f32[16,128]{1,0:T(8,128)S(1)}, f32[16,128]{1,0:T(8,128)}, u32[]{:S(2)}) copy-start(f32[16,128]{1,0:T(8,128)} %param.22) | copy-start | bytes 24580
  216.8 16.1 %collective-permute-start.6 = (f32[32,128]{1,0:T(8,128)S(1)}, f32[32,128]{1,0:T(8,128)S(1)}, u32[]{:S(2)}, u32[]{:S(2)}) collective-permute-start(f32[32,128]{1,0:T(8,128)S(1)} %multiply_add_fusion.4), channel_id=1, source_target_pairs={{0,4},{4,8},{8,12},{12,16},{16,20},{20,24},{24,28},{28,32},{32,36}... | collective-permute-start | bytes 49160 | tf_op jit(solution)/shard_map/ppermute | solution.py:20
  218.8 14.2 %collective-permute-start.7 = (f32[32,128]{1,0:T(8,128)S(1)}, f32[32,128]{1,0:T(8,128)S(1)}, u32[]{:S(2)}, u32[]{:S(2)}) collective-permute-start(f32[32,128]{1,0:T(8,128)S(1)} %multiply_add_fusion.4), channel_id=1, source_target_pairs={{4,0},{8,4},{12,8},{16,12},{20,16},{24,20},{28,24},{32,28},{36,32}... | collective-permute-start | bytes 49160 | tf_op jit(solution)/shard_map/ppermute | solution.py:21
  316.9 8.1 %collective-permute-start.8 = (f32[32,128]{1,0:T(8,128)S(1)}, f32[32,128]{1,0:T(8,128)S(1)}, u32[]{:S(2)}, u32[]{:S(2)}) collective-permute-start(f32[32,128]{1,0:T(8,128)S(1)} %add.119), channel_id=1, source_target_pairs={{0,4},{4,8},{8,12},{12,16},{16,20},{20,24},{24,28},{28,32},{32,36}... | collective-permute-start | bytes 49160 | tf_op jit(solution)/shard_map/ppermute | solution.py:20
  318.8 7.2 %collective-permute-start.9 = (f32[32,128]{1,0:T(8,128)S(1)}, f32[32,128]{1,0:T(8,128)S(1)}, u32[]{:S(2)}, u32[]{:S(2)}) collective-permute-start(f32[32,128]{1,0:T(8,128)S(1)} %add.119), channel_id=1, source_target_pairs={{4,0},{8,4},{12,8},{16,12},{20,16},{24,20},{28,24},{32,28},{36,32}... | collective-permute-start | bytes 49160 | tf_op jit(solution)/shard_map/ppermute | solution.py:21
  339.4 7.7 %collective-permute-start.10 = (f32[32,128]{1,0:T(8,128)S(1)}, f32[32,128]{1,0:T(8,128)S(1)}, u32[]{:S(2)}, u32[]{:S(2)}) collective-permute-start(f32[32,128]{1,0:T(8,128)S(1)} %multiply_add_fusion.3), channel_id=1, source_target_pairs={{0,4},{4,8},{8,12},{12,16},{16,20},{20,24},{24,28},{28,32},{32,36}... | collective-permute-start | bytes 49160 | tf_op jit(solution)/shard_map/ppermute | solution.py:20
  341.3 7.2 %collective-permute-start.11 = (f32[32,128]{1,0:T(8,128)S(1)}, f32[32,128]{1,0:T(8,128)S(1)}, u32[]{:S(2)}, u32[]{:S(2)}) collective-permute-start(f32[32,128]{1,0:T(8,128)S(1)} %multiply_add_fusion.3), channel_id=1, source_target_pairs={{4,0},{8,4},{12,8},{16,12},{20,16},{24,20},{28,24},{32,28},{36,32}... | collective-permute-start | bytes 49160 | tf_op jit(solution)/shard_map/ppermute | solution.py:21
  365.4 10.0 %collective-permute-start.12 = (f32[32,128]{1,0:T(8,128)S(1)}, f32[32,128]{1,0:T(8,128)S(1)}, u32[]{:S(2)}, u32[]{:S(2)}) collective-permute-start(f32[32,128]{1,0:T(8,128)S(1)} %add.124), channel_id=1, source_target_pairs={{0,1},{1,2},{2,3},{3,4},{4,5},{5,6},{6,7},{7,8},{8,9},{9,10},{10,1... | collective-permute-start | bytes 49160 | tf_op jit(solution)/shard_map/ppermute | solution.py:20
  368.6 8.0 %collective-permute-start.13 = (f32[32,128]{1,0:T(8,128)S(1)}, f32[32,128]{1,0:T(8,128)S(1)}, u32[]{:S(2)}, u32[]{:S(2)}) collective-permute-start(f32[32,128]{1,0:T(8,128)S(1)} %add.124), channel_id=1, source_target_pairs={{1,0},{2,1},{3,2},{4,3},{5,4},{6,5},{7,6},{8,7},{9,8},{10,9},{11,1... | collective-permute-start | bytes 49160 | tf_op jit(solution)/shard_map/ppermute | solution.py:21
  390.0 9.8 %collective-permute-start.14 = (f32[32,128]{1,0:T(8,128)S(1)}, f32[32,128]{1,0:T(8,128)S(1)}, u32[]{:S(2)}, u32[]{:S(2)}) collective-permute-start(f32[32,128]{1,0:T(8,128)S(1)} %multiply_add_fusion.1), channel_id=1, source_target_pairs={{0,1},{1,2},{2,3},{3,4},{4,5},{5,6},{6,7},{7,8},{8,9},{9,10},{10,1... | collective-permute-start | bytes 49160 | tf_op jit(solution)/shard_map/ppermute | solution.py:20
  391.9 9.3 %collective-permute-start.15 = (f32[32,128]{1,0:T(8,128)S(1)}, f32[32,128]{1,0:T(8,128)S(1)}, u32[]{:S(2)}, u32[]{:S(2)}) collective-permute-start(f32[32,128]{1,0:T(8,128)S(1)} %multiply_add_fusion.1), channel_id=1, source_target_pairs={{1,0},{2,1},{3,2},{4,3},{5,4},{6,5},{7,6},{8,7},{9,8},{10,9},{11,1... | collective-permute-start | bytes 49160 | tf_op jit(solution)/shard_map/ppermute | solution.py:21
  (3 other events, 162.1 us)
Sparse Core Ops, SparseCore 0:
  9.7 103.1 all-gather.3
  114.5 32.0 all-gather.5
where the time goes:
time: 428 us; the launch traced here: 422 us
  matrix products  123 us (29%)
  waiting for transfers between devices  99.6 us (23%)
  blocking collectives  98.5 us (23%)
  starting transfers between devices  70.5 us (16%)
  between operations  15.4 us (4%)
  other arithmetic  8.12 us (2%)
  local copies, waits for them, and re-layouts  7.38 us (2%)
    dot_general x9, matrix products, tile_product(): jnp.einsum('bkij,bkj->bi', tiles, stacked, precision=highest)  108 us
    all_gather x1, waiting for transfers between devices, shards(): lax.all_gather(tiles1, 'row', axis=0, tiled=True)  90.5 us
    psum x1, blocking collectives, shards(): right2 = lax.psum(term2, 'wa')  54 us
    ppermute x8, starting transfers between devices, with_halo(): after = lax.ppermute(leading, axis, down)  52.4 us
    ppermute x8, starting transfers between devices, with_halo(): before = lax.ppermute(last, axis, up)  18.1 us
    psum x1, blocking collectives, shards(): right1 = lax.psum(term1, 'row')  14.3 us
    all_gather x1, blocking collectives, shards(): lax.all_gather(diag1, 'row', axis=0, tiled=True)  12.1 us
    all_gather x1, blocking collectives, shards(): lax.all_gather(cols1, 'row', axis=0, tiled=True)  11.2 us
  transfers between devices with their start and end apart: 18, of which 7 were waited for; matrix products, arithmetic and copies ran while one was open for 15% of the time, Pallas kernels for 0%

commit v1 on v0

v1 whole, which is shorter than its diff:
```python
import functools

import jax
import jax.numpy as jnp
from jax import lax
from jax.experimental import pallas as pl
from jax.experimental.pallas import tpu as pltpu
from jax.sharding import PartitionSpec as P

MESH = pl.DeviceIdType.MESH
TILE = 128
KN = 4
R0 = 32
R1 = 8
NB2 = 16
ROWS = 4
RING = 128
relax = 0.8


def position():
    group, row = lax.axis_index("wa"), lax.axis_index("row")
    return group * ROWS + row, group, row


def along(device, offset, count):
    place = lax.rem(device + (offset + count), count)
    return lax.div(place, ROWS), lax.rem(place, ROWS)


def plane_peers(group, row, planes):
    plane, core = lax.div(group, 2), lax.rem(group, 2)
    return [(lax.rem(plane + step, planes) * 2 + core, row) for step in range(1, planes)]


def chip_line_peers(group, row):
    core = lax.rem(group, 2)
    out = []
    for step in range(1, 2 * ROWS):
        flip, shift = divmod(step, ROWS)
        out.append((group - core + lax.rem(core + flip, 2), lax.rem(row + shift, ROWS)))
    return out


def lane_sums(products):
    return jnp.sum(products, axis=1, keepdims=True)


def eye_mask():
    shape = (TILE, TILE)
    return lax.broadcasted_iota(jnp.int32, shape, 0) == lax.broadcasted_iota(jnp.int32, shape, 1)


def lanes():
    return lax.broadcasted_iota(jnp.int32, (TILE, TILE), 1)


def row_products(tiles, field, cols, own, b):
    last = field.shape[0] - 1
    total = tiles[b, 0] * field[pl.ds(own + b, 1), :]
    for k in range(KN):
        total = total + tiles[b, k + 1] * field[pl.ds(cols[b, k] & last, 1), :]
    return total


def level_apply(tiles, field, cols, own, count, unroll):
    lane = lanes()

    def step(b, columns):
        return jnp.where(lane == b, lane_sums(row_products(tiles, field, cols, own, b)), columns)

    columns = lax.fori_loop(0, count, step, jnp.zeros((TILE, TILE), jnp.float32), unroll=unroll)
    return columns.T[:count]


def prolong(interp, coarse, owner, count, unroll):
    lane, last = lanes(), coarse.shape[0] - 1

    def step(b, columns):
        products = interp[b] * coarse[pl.ds(owner[b] & last, 1), :]
        return jnp.where(lane == b, lane_sums(products), columns)

    columns = lax.fori_loop(0, count, step, jnp.zeros((TILE, TILE), jnp.float32), unroll=unroll)
    return columns.T[:count]


def restrict(tiles, field, cols, own, rest, interp, owner, count, targets, unroll):
    eye = eye_mask()
    place = lax.broadcasted_iota(jnp.int32, (targets, TILE), 0)

    def step(b, sums):
        products = row_products(tiles, field, cols, own, b)
        residual = lane_sums(jnp.where(eye, rest[pl.ds(b, 1), :], 0.0) - products)
        lifted = jnp.sum(interp[b] * residual, axis=0, keepdims=True)
        return sums + jnp.where(place == owner[b] & (targets - 1), lifted, 0.0)

    return lax.fori_loop(0, count, step, jnp.zeros((targets, TILE), jnp.float32), unroll=unroll)


def diagonals(tiles, out, count, unroll):
    eye = eye_mask()

    def step(b, carry):
        out[pl.ds(b, 1), :] = jnp.sum(jnp.where(eye, tiles[b, 0], 0.0), axis=0, keepdims=True)
        return carry

    lax.fori_loop(0, count, step, 0, unroll=unroll)


def kernel(
    groups,
    rhs_hbm, tiles0_hbm, diag0_hbm, cols0_hbm, tiles1_hbm, diag1_hbm, cols1_hbm,
    tiles2_hbm, diag2_hbm, cols2_hbm, interp0_hbm, owner0_hbm, interp1_hbm, owner1_hbm,
    out0, out1, out2,
    rhs, tiles0, diag0, cols0, tiles1, diag1, cols1,
    tiles2, diag2, cols2, interp0, owner0, interp1, owner1,
    scale0, scale1, scale2, rest0, rest1, field2,
    fine_a, fine_b, fine_c, fine_d, mid_s, mid_a, mid_b, mid_c, mid_d,
    partial, parts, near, far,
    load_sem, send_sem, recv_sem,
):
    devices = groups * ROWS
    planes = groups // 2
    device, group, row = position()
    core = lax.rem(group, 2)
    plane = lax.div(group, 2)

    base0 = pl.multiple_of(lax.rem(device * R0, RING), R0)
    base1 = pl.multiple_of(lax.rem(device * R1, RING), R1)
    own0, own1 = pl.ds(base0, R0), pl.ds(base1, R1)

    own_tiles = pl.ds(0, 1)
    other_tiles = pl.ds(1, KN)

    def load(index, source, target):
        return pltpu.make_async_copy(source, target, load_sem.at[index])

    first = [
        load(0, tiles0_hbm.at[:, own_tiles], tiles0.at[:, own_tiles]),
        load(1, diag0_hbm, diag0),
        load(2, rhs_hbm, rhs),
        load(3, tiles1_hbm.at[:, own_tiles], tiles1.at[:, own_tiles]),
        load(4, diag1_hbm, diag1),
    ]
    fine = [
        load(5, tiles0_hbm.at[:, other_tiles], tiles0.at[:, other_tiles]),
        load(6, cols0_hbm, cols0),
        load(7, interp0_hbm, interp0),
        load(8, owner0_hbm, owner0),
    ]
    middle = [
        load(9, tiles1_hbm.at[:, other_tiles], tiles1.at[:, other_tiles]),
        load(10, cols1_hbm, cols1),
        load(11, interp1_hbm, interp1),
        load(12, owner1_hbm, owner1),
    ]
    coarse = [
        load(13, tiles2_hbm, tiles2),
        load(14, diag2_hbm, diag2),
        load(15, cols2_hbm, cols2),
    ]
    for copy in first:
        copy.start()

    around = [
        (lax.rem(group + side + groups, groups), place) for side in (-1, 1) for place in range(ROWS)
    ]
    mates = [(group, lax.rem(row + step, ROWS)) for step in range(1, ROWS)]
    far_peers = plane_peers(group, row, planes)
    barrier = pltpu.get_barrier_semaphore()
    greeted = around + mates + far_peers
    for peer in greeted:
        pl.semaphore_signal(barrier, inc=1, device_id=peer, device_id_type=MESH)

    for copy in first:
        copy.wait()
    for copy in fine + middle + coarse:
        copy.start()

    def send(index, source, target, peer):
        pltpu.make_async_remote_copy(
            src_ref=source, dst_ref=target, send_sem=send_sem.at[index], recv_sem=recv_sem.at[index],
            device_id=peer, device_id_type=MESH,
        ).start()

    def arrivals(index, like):
        return pltpu.make_async_remote_copy(
            src_ref=like, dst_ref=like, send_sem=send_sem.at[index], recv_sem=recv_sem.at[index],
            device_id=mates[0], device_id_type=MESH,
        )

    def send_fine(index, field):
        own = field.at[own0]
        for step in (1, -1):
            send(index, own, own, along(device, step, devices))

    def send_middle(index, field):
        own = field.at[own1]
        for step in (4, -4, 3, -3, 2, -2, 1, -1):
            send(index, own, own, along(device, step, devices))

    def fine_wait(index, field):
        arrivals(index, field.at[pl.ds(0, 2 * R0)]).wait_recv()

    def middle_wait(index, field):
        arrivals(index, field.at[pl.ds(0, 2 * R0)]).wait_recv()

    diagonals(tiles0, scale0, R0, 4)
    scale0[...] = relax / (diag0[...] + scale0[...])
    fine_a[own0, :] = rhs[...] * scale0[...]
    diagonals(tiles1, scale1, R1, 4)
    mid_s[own1, :] = relax / (diag1[...] + scale1[...])
    pl.semaphore_wait(barrier, len(greeted))
    send_fine(0, fine_a)
    send_middle(1, mid_s)

    def apply0(field):
        return level_apply(tiles0, field, cols0, base0, R0, 4)

    def sweep0(field):
        v = field[own0, :]
        return v + scale0[...] * (rhs[...] - diag0[...] * v - apply0(field))

    for copy in fine:
        copy.wait()
    fine_wait(0, fine_a)
    fine_b[own0, :] = sweep0(fine_a)
    send_fine(2, fine_b)
    rest0[...] = rhs[...] - diag0[...] * fine_b[own0, :]
    fine_wait(2, fine_b)
    part = restrict(tiles0, fine_b, cols0, base0, rest0, interp0, owner0, R0, R0, 4)

    partial[...] = part
    slot = row * (3 * R0)
    parts[pl.ds(slot + R0, R0), :] = part
    for place in range(ROWS):
        low = R1 * place
        send(3, partial.at[pl.ds(low, R0 - low)], parts.at[pl.ds(slot + low, R0 - low)],
             (lax.rem(group + 1, groups), place))
        send(3, partial.at[pl.ds(0, low + R1)], parts.at[pl.ds(slot + 2 * R0, low + R1)],
             (lax.rem(group + groups - 1, groups), place))
    for mate in mates:
        send(3, partial, parts.at[pl.ds(slot + R0, R0)], mate)
    for copy in middle:
        copy.wait()
    middle_wait(1, mid_s)
    arrivals(3, parts.at[pl.ds(0, 8 * R0)]).wait_recv()
    for block in range(2 * ROWS + 1):
        offset = (row + block) * R1
        right = parts[pl.ds(offset, R1), :]
        for place in range(1, ROWS):
            right = right + parts[pl.ds(offset + place * 3 * R0, R1), :]
        there = pl.ds(pl.multiple_of(lax.rem((device + (devices + block - ROWS)) * R1, RING), R1), R1)
        mid_a[there, :] = right * mid_s[there, :]
        if block == ROWS:
            right1 = right
    s1 = mid_s[own1, :]

    def sweep1(field):
        v = field[own1, :]
        return v + s1 * (right1 - diag1[...] * v - level_apply(tiles1, field, cols1, base1, R1, 4))

    mid_b[own1, :] = sweep1(mid_a)
    send_middle(4, mid_b)
    rest1[...] = right1 - diag1[...] * mid_b[own1, :]
    middle_wait(4, mid_b)
    part2 = restrict(tiles1, mid_b, cols1, base1, rest1, interp1, owner1, R1, NB2, 4)

    line_slot = core * ROWS + row
    near[line_slot] = part2
    for peer in chip_line_peers(group, row):
        send(5, near.at[line_slot], near.at[line_slot], peer)
    for copy in coarse:
        copy.wait()
    diagonals(tiles2, scale2, NB2, 4)
    scale2[...] = relax / (diag2[...] + scale2[...])
    arrivals(5, near.at[pl.ds(0, 2 * ROWS - 1)]).wait_recv()
    total = near[0]
    for place in range(1, 2 * ROWS):
        total = total + near[place]
    far[plane] = total
    for peer in far_peers:
        send(6, far.at[plane], far.at[plane], peer)
    arrivals(6, far.at[pl.ds(0, planes - 1)]).wait_recv()
    right2 = far[0]
    for place in range(1, planes):
        right2 = right2 + far[place]

    v2 = right2 * scale2[...]
    field2[...] = v2
    v2 = v2 + scale2[...] * (right2 - diag2[...] * v2 - level_apply(tiles2, field2, cols2, 0, NB2, 4))
    out2[...] = v2

    mid_c[own1, :] = mid_b[own1, :] + prolong(interp1, out2, owner1, R1, 4)
    send_middle(7, mid_c)
    middle_wait(7, mid_c)
    mid_d[own1, :] = sweep1(mid_c)
    send_middle(8, mid_d)
    middle_wait(8, mid_d)
    place1 = pl.ds(row * R1, R1)
    out1[place1, :] = sweep1(mid_d)
    for mate in mates:
        send(9, out1.at[place1], out1.at[place1], mate)
    arrivals(9, out1.at[pl.ds(0, R0 - R1)]).wait_recv()

    fine_c[own0, :] = fine_b[own0, :] + prolong(interp0, out1, owner0, R0, 4)
    send_fine(10, fine_c)
    fine_wait(10, fine_c)
    fine_d[own0, :] = sweep0(fine_c)
    send_fine(11, fine_d)
    fine_wait(11, fine_d)
    out0[...] = sweep0(fine_d)

    for index, like in (
        (0, fine_a.at[pl.ds(0, 2 * R0)]), (1, mid_s.at[pl.ds(0, 2 * R0)]), (2, fine_b.at[pl.ds(0, 2 * R0)]),
        (3, parts.at[pl.ds(0, 8 * R0)]), (4, mid_b.at[pl.ds(0, 2 * R0)]), (5, near.at[pl.ds(0, 2 * ROWS - 1)]),
        (6, far.at[pl.ds(0, planes - 1)]), (7, mid_c.at[pl.ds(0, 2 * R0)]), (8, mid_d.at[pl.ds(0, 2 * R0)]),
        (9, out1.at[pl.ds(0, R0 - R1)]), (10, fine_c.at[pl.ds(0, 2 * R0)]), (11, fine_d.at[pl.ds(0, 2 * R0)]),
    ):
        arrivals(index, like).wait_send()


def shards(groups, *arguments):
    f32 = jnp.float32
    vmem = lambda *shape: pltpu.VMEM(shape, f32)
    copies = []
    for index, argument in enumerate(arguments):
        space = pltpu.SMEM if argument.dtype == jnp.int32 else pltpu.VMEM
        copies.append(space(argument.shape, argument.dtype))
    scratch = copies + [
        vmem(R0, TILE), vmem(R1, TILE), vmem(NB2, TILE), vmem(R0, TILE), vmem(R1, TILE), vmem(NB2, TILE),
        *(vmem(RING, TILE) for _ in range(9)),
        vmem(R0, TILE), vmem(ROWS * 3 * R0, TILE), vmem(2 * ROWS, NB2, TILE), vmem(groups // 2, NB2, TILE),
        pltpu.SemaphoreType.DMA((16,)), pltpu.SemaphoreType.DMA((12,)), pltpu.SemaphoreType.DMA((12,)),
    ]
    return pl.pallas_call(
        functools.partial(kernel, groups),
        out_shape=tuple(jax.ShapeDtypeStruct((n, TILE), f32) for n in (R0, R0, NB2)),
        in_specs=[pl.BlockSpec(memory_space=pl.ANY)] * len(arguments),
        out_specs=(pl.BlockSpec(memory_space=pltpu.VMEM),) * 3,
        scratch_shapes=scratch,
        compiler_params=pltpu.CompilerParams(
            collective_id=0, has_side_effects=True, vmem_limit_bytes=56 * 2**20
        ),
        name="vcycle",
    )(*arguments)


def solution(mesh):
    both = ("wa", "row")
    in_specs = (
        P(both, None),
        P(both, None, None, None),
        P(both, None),
        P(both, None),
        P(both, None, None, None),
        P(both, None),
        P(both, None),
        P(),
        P(),
        P(),
        P(both, None, None),
        P(both),
        P(both, None, None),
        P(both),
    )
    out_specs = (P(both, None), P("wa", None), P())
    return jax.shard_map(
        functools.partial(shards, mesh.shape["wa"]), mesh=mesh, in_specs=in_specs, out_specs=out_specs, check_vma=False
    )
```

time: 428 us -> 77.7 us (0.18)
  the two profiles are of different devices: /device:TPU:8 before, /device:TPU:0 now
where the time goes in v1:
time: 77.7 us; the launch traced here: 77.3 us
  Pallas kernels  68.6 us (88%)
  local copies, waits for them, and re-layouts  8.01 us (10%)
    pallas_call x1, Pallas kernels, shards(): pl.pallas_call(functools.partial(kernel, groups), out_shape=tuple((jax.Sh...  68.6 us
    unnamed x6, local copies, waits for them, and re-layouts  8.01 us

profile of v1, /device:TPU:0, one launch (start us, length us, event | category | flops | bytes accessed | tf_op | source)
XLA Modules:
  0.0 77.3 jit_solution(6412140798142906010)
XLA Ops:
  0.6 1.3 %copy.18.cols1_hbm = s32[8,4]{1,0:T(8,128)} copy(s32[8,4]{0,1:T(4,128)} %param.20) | data formatting | bytes 256 | tf_op args[6]
  2.0 1.4 %copy.19.cols2_hbm = s32[16,4]{1,0:T(8,128)} copy(s32[16,4]{0,1:T(4,128)} %param.23) | data formatting | bytes 512 | tf_op args[9]
  3.3 1.4 %copy.17.cols0_hbm = s32[32,4]{1,0:T(8,128)} copy(s32[32,4]{0,1:T(4,128)} %param.17) | data formatting | bytes 1024 | tf_op args[3]
  4.7 68.6 %vcycle.1 = (f32[32,128]{1,0:T(8,128)}, f32[32,128]{1,0:T(8,128)}, f32[16,128]{1,0:T(8,128)}) custom-call(f32[32,128]{1,0:T(8,128)} %rhs_hbm.1, f32[32,5,128,128]{3,2,1,0:T(8,128)} %tiles0_hbm.1, f32[32,128]{1,0:T(8,128)} %diag0_hbm.1, s32[32,4]{1,0:T(8,128)} %copy.17.cols0_hbm, f32[8,5,128,128]{3,2,1,0:T(8,128)} %tiles1_hbm.1, f32[8,128]{1,0:T(8,128)} %diag1_hbm.1, ...), custom_call_target="tpu_custom_call" | custom-call | tf_op jit(solution)/shard_map/vcycle/pallas_call | solution.py:336
  73.3 1.3 %copy.23 = f32[32,128]{1,0:T(8,128)} copy(f32[32,128]{1,0:T(8,128)} %get-tuple-element.6) | data formatting | bytes 32768
  74.7 1.3 %copy.24 = f32[32,128]{1,0:T(8,128)} copy(f32[32,128]{1,0:T(8,128)} %get-tuple-element.7) | data formatting | bytes 32768
  76.0 1.3 %copy.25 = f32[16,128]{1,0:T(8,128)} copy(f32[16,128]{1,0:T(8,128)} %get-tuple-element.8) | data formatting | bytes 16384

commit v2 on v1

--- a/solution.py
+++ b/solution.py
@@ -59,7 +59,7 @@
     last = field.shape[0] - 1
     total = tiles[b, 0] * field[pl.ds(own + b, 1), :]
     for k in range(KN):
-        total = total + tiles[b, k + 1] * field[pl.ds(cols[b, k] & last, 1), :]
+        total = total + tiles[b, k + 1] * field[pl.ds(cols[k, b] & last, 1), :]
     return total
 
 
@@ -139,25 +139,24 @@
         load(0, tiles0_hbm.at[:, own_tiles], tiles0.at[:, own_tiles]),
         load(1, diag0_hbm, diag0),
         load(2, rhs_hbm, rhs),
-        load(3, tiles1_hbm.at[:, own_tiles], tiles1.at[:, own_tiles]),
-        load(4, diag1_hbm, diag1),
     ]
     fine = [
-        load(5, tiles0_hbm.at[:, other_tiles], tiles0.at[:, other_tiles]),
-        load(6, cols0_hbm, cols0),
-        load(7, interp0_hbm, interp0),
-        load(8, owner0_hbm, owner0),
+        load(3, cols0_hbm, cols0),
+        load(4, tiles0_hbm.at[:, other_tiles], tiles0.at[:, other_tiles]),
     ]
     middle = [
-        load(9, tiles1_hbm.at[:, other_tiles], tiles1.at[:, other_tiles]),
-        load(10, cols1_hbm, cols1),
-        load(11, interp1_hbm, interp1),
-        load(12, owner1_hbm, owner1),
+        load(5, tiles1_hbm, tiles1),
+        load(6, diag1_hbm, diag1),
+        load(7, cols1_hbm, cols1),
+        load(8, interp0_hbm, interp0),
+        load(9, owner0_hbm, owner0),
     ]
     coarse = [
-        load(13, tiles2_hbm, tiles2),
-        load(14, diag2_hbm, diag2),
-        load(15, cols2_hbm, cols2),
+        load(10, interp1_hbm, interp1),
+        load(11, owner1_hbm, owner1),
+        load(12, tiles2_hbm, tiles2),
+        load(13, diag2_hbm, diag2),
+        load(14, cols2_hbm, cols2),
     ]
     for copy in first:
         copy.start()
@@ -174,7 +173,7 @@
 
     for copy in first:
         copy.wait()
-    for copy in fine + middle + coarse:
+    for copy in fine:
         copy.start()
 
     def send(index, source, target, peer):
@@ -208,14 +207,11 @@
     diagonals(tiles0, scale0, R0, 4)
     scale0[...] = relax / (diag0[...] + scale0[...])
     fine_a[own0, :] = rhs[...] * scale0[...]
-    diagonals(tiles1, scale1, R1, 4)
-    mid_s[own1, :] = relax / (diag1[...] + scale1[...])
     pl.semaphore_wait(barrier, len(greeted))
     send_fine(0, fine_a)
-    send_middle(1, mid_s)
 
     def apply0(field):
-        return level_apply(tiles0, field, cols0, base0, R0, 4)
+        return level_apply(tiles0, field, cols0, base0, R0, 16)
 
     def sweep0(field):
         v = field[own0, :]
@@ -223,12 +219,19 @@
 
     for copy in fine:
         copy.wait()
+    for copy in middle + coarse:
+        copy.start()
     fine_wait(0, fine_a)
     fine_b[own0, :] = sweep0(fine_a)
     send_fine(2, fine_b)
     rest0[...] = rhs[...] - diag0[...] * fine_b[own0, :]
+    for copy in middle:
+        copy.wait()
+    diagonals(tiles1, scale1, R1, 8)
+    mid_s[own1, :] = relax / (diag1[...] + scale1[...])
+    send_middle(1, mid_s)
     fine_wait(2, fine_b)
-    part = restrict(tiles0, fine_b, cols0, base0, rest0, interp0, owner0, R0, R0, 4)
+    part = restrict(tiles0, fine_b, cols0, base0, rest0, interp0, owner0, R0, R0, 8)
 
     partial[...] = part
     slot = row * (3 * R0)
@@ -241,8 +244,6 @@
              (lax.rem(group + groups - 1, groups), place))
     for mate in mates:
         send(3, partial, parts.at[pl.ds(slot + R0, R0)], mate)
-    for copy in middle:
-        copy.wait()
     middle_wait(1, mid_s)
     arrivals(3, parts.at[pl.ds(0, 8 * R0)]).wait_recv()
     for block in range(2 * ROWS + 1):
@@ -258,22 +259,22 @@
 
     def sweep1(field):
         v = field[own1, :]
-        return v + s1 * (right1 - diag1[...] * v - level_apply(tiles1, field, cols1, base1, R1, 4))
+        return v + s1 * (right1 - diag1[...] * v - level_apply(tiles1, field, cols1, base1, R1, 8))
 
     mid_b[own1, :] = sweep1(mid_a)
     send_middle(4, mid_b)
     rest1[...] = right1 - diag1[...] * mid_b[own1, :]
+    for copy in coarse:
+        copy.wait()
+    diagonals(tiles2, scale2, NB2, 8)
+    scale2[...] = relax / (diag2[...] + scale2[...])
     middle_wait(4, mid_b)
-    part2 = restrict(tiles1, mid_b, cols1, base1, rest1, interp1, owner1, R1, NB2, 4)
+    part2 = restrict(tiles1, mid_b, cols1, base1, rest1, interp1, owner1, R1, NB2, 8)
 
     line_slot = core * ROWS + row
     near[line_slot] = part2
     for peer in chip_line_peers(group, row):
         send(5, near.at[line_slot], near.at[line_slot], peer)
-    for copy in coarse:
-        copy.wait()
-    diagonals(tiles2, scale2, NB2, 4)
-    scale2[...] = relax / (diag2[...] + scale2[...])
     arrivals(5, near.at[pl.ds(0, 2 * ROWS - 1)]).wait_recv()
     total = near[0]
     for place in range(1, 2 * ROWS):
@@ -288,10 +289,10 @@
 
     v2 = right2 * scale2[...]
     field2[...] = v2
-    v2 = v2 + scale2[...] * (right2 - diag2[...] * v2 - level_apply(tiles2, field2, cols2, 0, NB2, 4))
+    v2 = v2 + scale2[...] * (right2 - diag2[...] * v2 - level_apply(tiles2, field2, cols2, 0, NB2, 16))
     out2[...] = v2
 
-    mid_c[own1, :] = mid_b[own1, :] + prolong(interp1, out2, owner1, R1, 4)
+    mid_c[own1, :] = mid_b[own1, :] + prolong(interp1, out2, owner1, R1, 8)
     send_middle(7, mid_c)
     middle_wait(7, mid_c)
     mid_d[own1, :] = sweep1(mid_c)
@@ -303,7 +304,7 @@
         send(9, out1.at[place1], out1.at[place1], mate)
     arrivals(9, out1.at[pl.ds(0, R0 - R1)]).wait_recv()
 
-    fine_c[own0, :] = fine_b[own0, :] + prolong(interp0, out1, owner0, R0, 4)
+    fine_c[own0, :] = fine_b[own0, :] + prolong(interp0, out1, owner0, R0, 16)
     send_fine(10, fine_c)
     fine_wait(10, fine_c)
     fine_d[own0, :] = sweep0(fine_c)
@@ -320,8 +321,18 @@
         arrivals(index, like).wait_send()
 
 
+def hand_over(*refs):
+    sources, targets, sems = refs[:3], refs[3:6], refs[6]
+    copies = [pltpu.make_async_copy(sources[i], targets[i], sems.at[i]) for i in range(3)]
+    for copy in copies:
+        copy.start()
+    for copy in copies:
+        copy.wait()
+
+
 def shards(groups, *arguments):
     f32 = jnp.float32
+    arguments = [a.T if a.dtype == jnp.int32 and a.ndim == 2 else a for a in arguments]
     vmem = lambda *shape: pltpu.VMEM(shape, f32)
     copies = []
     for index, argument in enumerate(arguments):
@@ -333,9 +344,10 @@
         vmem(R0, TILE), vmem(ROWS * 3 * R0, TILE), vmem(2 * ROWS, NB2, TILE), vmem(groups // 2, NB2, TILE),
         pltpu.SemaphoreType.DMA((16,)), pltpu.SemaphoreType.DMA((12,)), pltpu.SemaphoreType.DMA((12,)),
     ]
-    return pl.pallas_call(
+    out_shape = tuple(jax.ShapeDtypeStruct((n, TILE), f32) for n in (R0, R0, NB2))
+    results = pl.pallas_call(
         functools.partial(kernel, groups),
-        out_shape=tuple(jax.ShapeDtypeStruct((n, TILE), f32) for n in (R0, R0, NB2)),
+        out_shape=out_shape,
         in_specs=[pl.BlockSpec(memory_space=pl.ANY)] * len(arguments),
         out_specs=(pl.BlockSpec(memory_space=pltpu.VMEM),) * 3,
         scratch_shapes=scratch,
@@ -344,6 +356,14 @@
         ),
         name="vcycle",
     )(*arguments)
+    return pl.pallas_call(
+        hand_over,
+        out_shape=out_shape,
+        in_specs=[pl.BlockSpec(memory_space=pltpu.HBM)] * 3,
+        out_specs=(pl.BlockSpec(memory_space=pltpu.HBM),) * 3,
+        scratch_shapes=[pltpu.SemaphoreType.DMA((3,))],
+        name="results",
+    )(*results)
 
 
 def solution(mesh):

time: 77.7 us -> 69.5 us (0.89)
  local copies, waits for them, and re-layouts: 8.01 us -> 0 us
    unnamed x6 -> x0, local copies, waits for them, and re-layouts: 8.01 us -> none
    pallas_call x1 -> x2, Pallas kernels: 68.6 us -> 68.7 us  [the longest x1 66.3 us: shards(): pl.pallas_call(functools.partial(kernel, groups), out_shape=out_shape, in...]
where the time goes in v2:
time: 69.5 us; the launch traced here: 69.3 us
  Pallas kernels  68.7 us (99%)
    pallas_call x1, Pallas kernels, shards(): pl.pallas_call(functools.partial(kernel, groups), out_shape=out_shape, in...  66.3 us
    pallas_call x1, Pallas kernels, shards(): pl.pallas_call(hand_over, out_shape=out_shape, in_specs=[pl.BlockSpec(mem...  2.37 us

profile of v2, /device:TPU:0, one launch (start us, length us, event | category | flops | bytes accessed | tf_op | source)
XLA Modules:
  0.0 69.3 jit_solution(2045536426276138827)
XLA Ops:
  0.6 66.3 %vcycle.1 = (f32[32,128]{1,0:T(8,128)}, f32[32,128]{1,0:T(8,128)}, f32[16,128]{1,0:T(8,128)}) custom-call(f32[32,128]{1,0:T(8,128)} %rhs_hbm.1, f32[32,5,128,128]{3,2,1,0:T(8,128)} %tiles0_hbm.1, f32[32,128]{1,0:T(8,128)} %diag0_hbm.1, s32[4,32]{1,0:T(4,128)} %bitcast.3, f32[8,5,128,128]{3,2,1,0:T(8,128)} %tiles1_hbm.1, f32[8,128]{1,0:T(8,128)} %diag1_hbm.1, ...), custom_call_target="tpu_custom_call" | custom-call | tf_op jit(solution)/shard_map/vcycle/pallas_call | solution.py:348
  67.0 2.4 %results.1 = (f32[32,128]{1,0:T(8,128)}, f32[32,128]{1,0:T(8,128)}, f32[16,128]{1,0:T(8,128)}) custom-call(f32[32,128]{1,0:T(8,128)} %get-tuple-element.6.refs_0_, f32[32,128]{1,0:T(8,128)} %get-tuple-element.7.refs_1_, f32[16,128]{1,0:T(8,128)} %get-tuple-element.8.refs_2_), custom_call_target="tpu_custom_call" | custom-call | tf_op jit(solution)/shard_map/results/pallas_call | solution.py:359

commit v3 on v2

--- a/solution.py
+++ b/solution.py
@@ -28,6 +28,9 @@
     return lax.div(place, ROWS), lax.rem(place, ROWS)
 
 
+STEPS = (4, -4, 3, -3, 2, -2, 1, -1)
+
+
 def plane_peers(group, row, planes):
     plane, core = lax.div(group, 2), lax.rem(group, 2)
     return [(lax.rem(plane + step, planes) * 2 + core, row) for step in range(1, planes)]
@@ -55,41 +58,48 @@
     return lax.broadcasted_iota(jnp.int32, (TILE, TILE), 1)
 
 
-def row_products(tiles, field, cols, own, b):
-    last = field.shape[0] - 1
-    total = tiles[b, 0] * field[pl.ds(own + b, 1), :]
-    for k in range(KN):
-        total = total + tiles[b, k + 1] * field[pl.ds(cols[k, b] & last, 1), :]
-    return total
-
-
-def level_apply(tiles, field, cols, own, count, unroll):
+def block_rows(products, count, unroll):
     lane = lanes()
 
     def step(b, columns):
-        return jnp.where(lane == b, lane_sums(row_products(tiles, field, cols, own, b)), columns)
+        return jnp.where(lane == b, lane_sums(products(b)), columns)
 
     columns = lax.fori_loop(0, count, step, jnp.zeros((TILE, TILE), jnp.float32), unroll=unroll)
     return columns.T[:count]
 
 
+def own_products(tiles, field, own):
+    return lambda b: tiles[b, 0] * field[pl.ds(own + b, 1), :]
+
+
+def neighbour_products(tiles, field, cols):
+    last = field.shape[0] - 1
+
+    def products(b):
+        total = tiles[b, 1] * field[pl.ds(cols[0, b] & last, 1), :]
+        for k in range(1, KN):
+            total = total + tiles[b, k + 1] * field[pl.ds(cols[k, b] & last, 1), :]
+        return total
+
+    return products
+
+
+def all_products(tiles, field, cols, own):
+    mine, others = own_products(tiles, field, own), neighbour_products(tiles, field, cols)
+    return lambda b: mine(b) + others(b)
+
+
 def prolong(interp, coarse, owner, count, unroll):
-    lane, last = lanes(), coarse.shape[0] - 1
-
-    def step(b, columns):
-        products = interp[b] * coarse[pl.ds(owner[b] & last, 1), :]
-        return jnp.where(lane == b, lane_sums(products), columns)
-
-    columns = lax.fori_loop(0, count, step, jnp.zeros((TILE, TILE), jnp.float32), unroll=unroll)
-    return columns.T[:count]
-
-
-def restrict(tiles, field, cols, own, rest, interp, owner, count, targets, unroll):
+    last = coarse.shape[0] - 1
+    return block_rows(lambda b: interp[b] * coarse[pl.ds(owner[b] & last, 1), :], count, unroll)
+
+
+def restrict(products_of, rest, interp, owner, count, targets, unroll):
     eye = eye_mask()
     place = lax.broadcasted_iota(jnp.int32, (targets, TILE), 0)
 
     def step(b, sums):
-        products = row_products(tiles, field, cols, own, b)
+        products = products_of(b)
         residual = lane_sums(jnp.where(eye, rest[pl.ds(b, 1), :], 0.0) - products)
         lifted = jnp.sum(interp[b] * residual, axis=0, keepdims=True)
         return sums + jnp.where(place == owner[b] & (targets - 1), lifted, 0.0)
@@ -161,15 +171,27 @@
     for copy in first:
         copy.start()
 
-    around = [
-        (lax.rem(group + side + groups, groups), place) for side in (-1, 1) for place in range(ROWS)
-    ]
     mates = [(group, lax.rem(row + step, ROWS)) for step in range(1, ROWS)]
     far_peers = plane_peers(group, row, planes)
+    after, before = lax.rem(group + 1, groups), lax.rem(group + groups - 1, groups)
+    has_after, has_before = group < groups - 1, group > 0
+    inside = jnp.logical_and(has_after, has_before)
     barrier = pltpu.get_barrier_semaphore()
-    greeted = around + mates + far_peers
-    for peer in greeted:
-        pl.semaphore_signal(barrier, inc=1, device_id=peer, device_id_type=MESH)
+
+    def greet(peers):
+        for peer in peers:
+            pl.semaphore_signal(barrier, inc=1, device_id=peer, device_id_type=MESH)
+
+    @pl.when(has_after)
+    def _():
+        greet([(after, place) for place in range(ROWS)])
+
+    @pl.when(has_before)
+    def _():
+        greet([(before, place) for place in range(ROWS)])
+
+    greet(mates + far_peers)
+    greeted = len(mates + far_peers) + jnp.where(has_after, ROWS, 0) + jnp.where(has_before, ROWS, 0)
 
     for copy in first:
         copy.wait()
@@ -188,64 +210,121 @@
             device_id=mates[0], device_id_type=MESH,
         )
 
-    def send_fine(index, field):
-        own = field.at[own0]
-        for step in (1, -1):
-            send(index, own, own, along(device, step, devices))
-
-    def send_middle(index, field):
-        own = field.at[own1]
-        for step in (4, -4, 3, -3, 2, -2, 1, -1):
-            send(index, own, own, along(device, step, devices))
-
-    def fine_wait(index, field):
-        arrivals(index, field.at[pl.ds(0, 2 * R0)]).wait_recv()
-
-    def middle_wait(index, field):
-        arrivals(index, field.at[pl.ds(0, 2 * R0)]).wait_recv()
+    def exists(step):
+        return device < devices - step if step > 0 else device >= -step
+
+    def exchange(index, field, own, steps, rows):
+        mine, reach = field.at[own], max(steps)
+        interior = jnp.logical_and(exists(reach), exists(-reach))
+
+        def post(step):
+            send(index, mine, mine, along(device, step, devices))
+
+        @pl.when(interior)
+        def _():
+            for step in steps:
+                post(step)
+
+        @pl.when(jnp.logical_not(interior))
+        def _():
+            for step in steps:
+                pl.when(exists(step))(functools.partial(post, step))
+
+        def await_all(wait):
+            def several(count):
+                wait(arrivals(index, field.at[pl.ds(0, rows * count)]))
+
+            pl.when(interior)(functools.partial(several, 2 * reach))
+            for place in range(reach):
+                outer = jnp.logical_or(device == place, device == devices - 1 - place)
+                pl.when(outer)(functools.partial(several, reach + place))
+
+        finish.append(lambda: await_all(lambda copies: copies.wait_send()))
+        return lambda: await_all(lambda copies: copies.wait_recv())
+
+    def exchange_fine(index, field):
+        return exchange(index, field, own0, (1, -1), R0)
+
+    def exchange_middle(index, field):
+        return exchange(index, field, own1, STEPS, R1)
+
+    finish = []
 
     diagonals(tiles0, scale0, R0, 4)
     scale0[...] = relax / (diag0[...] + scale0[...])
     fine_a[own0, :] = rhs[...] * scale0[...]
-    pl.semaphore_wait(barrier, len(greeted))
-    send_fine(0, fine_a)
-
-    def apply0(field):
-        return level_apply(tiles0, field, cols0, base0, R0, 16)
-
-    def sweep0(field):
-        v = field[own0, :]
-        return v + scale0[...] * (rhs[...] - diag0[...] * v - apply0(field))
+    pl.semaphore_wait(barrier, greeted)
+    fine_a_here = exchange_fine(0, fine_a)
+
+    def rest_of(right, diag, tiles, field, own, count, unroll):
+        mine = block_rows(own_products(tiles, field, own.start), count, unroll)
+        return right - diag[...] * field[own, :] - mine
+
+    def sweep0(field, here):
+        started = field[own0, :] + scale0[...] * rest_of(rhs[...], diag0, tiles0, field, own0, R0, 16)
+        here()
+        return started - scale0[...] * block_rows(neighbour_products(tiles0, field, cols0), R0, 16)
 
     for copy in fine:
         copy.wait()
     for copy in middle + coarse:
         copy.start()
-    fine_wait(0, fine_a)
-    fine_b[own0, :] = sweep0(fine_a)
-    send_fine(2, fine_b)
-    rest0[...] = rhs[...] - diag0[...] * fine_b[own0, :]
+    fine_b[own0, :] = sweep0(fine_a, fine_a_here)
+    fine_b_here = exchange_fine(2, fine_b)
+    rest0[...] = rest_of(rhs[...], diag0, tiles0, fine_b, own0, R0, 16)
     for copy in middle:
         copy.wait()
     diagonals(tiles1, scale1, R1, 8)
     mid_s[own1, :] = relax / (diag1[...] + scale1[...])
-    send_middle(1, mid_s)
-    fine_wait(2, fine_b)
-    part = restrict(tiles0, fine_b, cols0, base0, rest0, interp0, owner0, R0, R0, 8)
+    mid_s_here = exchange_middle(1, mid_s)
+    fine_b_here()
+    part = restrict(neighbour_products(tiles0, fine_b, cols0), rest0, interp0, owner0, R0, R0, 8)
 
     partial[...] = part
     slot = row * (3 * R0)
     parts[pl.ds(slot + R0, R0), :] = part
-    for place in range(ROWS):
-        low = R1 * place
-        send(3, partial.at[pl.ds(low, R0 - low)], parts.at[pl.ds(slot + low, R0 - low)],
-             (lax.rem(group + 1, groups), place))
-        send(3, partial.at[pl.ds(0, low + R1)], parts.at[pl.ds(slot + 2 * R0, low + R1)],
-             (lax.rem(group + groups - 1, groups), place))
+
+    @pl.when(has_after)
+    def _():
+        for place in range(ROWS):
+            low = R1 * place
+            send(3, partial.at[pl.ds(low, R0 - low)], parts.at[pl.ds(slot + low, R0 - low)], (after, place))
+
+    @pl.when(has_before)
+    def _():
+        for place in range(ROWS):
+            low = R1 * place
+            send(3, partial.at[pl.ds(0, low + R1)], parts.at[pl.ds(slot + 2 * R0, low + R1)], (before, place))
+
     for mate in mates:
         send(3, partial, parts.at[pl.ds(slot + R0, R0)], mate)
-    middle_wait(1, mid_s)
-    arrivals(3, parts.at[pl.ds(0, 8 * R0)]).wait_recv()
+
+    mate_rows = (ROWS - 1) * R0
+
+    def parts_received():
+        @pl.when(inside)
+        def _():
+            arrivals(3, parts.at[pl.ds(0, mate_rows + ROWS * (R0 + R1))]).wait_recv()
+
+        for place in range(ROWS):
+            @pl.when(jnp.logical_and(jnp.logical_not(has_before), row == place))
+            def _():
+                arrivals(3, parts.at[pl.ds(0, mate_rows + ROWS * R1 * (place + 1))]).wait_recv()
+
+            @pl.when(jnp.logical_and(jnp.logical_not(has_after), row == place))
+            def _():
+                arrivals(3, parts.at[pl.ds(0, mate_rows + ROWS * (R0 - R1 * place))]).wait_recv()
+
+    def parts_sent():
+        one_side = sum(R1 * (place + 1) for place in range(ROWS))
+        for sides, there in ((2, inside), (1, jnp.logical_not(inside))):
+            @pl.when(there)
+            def _():
+                arrivals(3, parts.at[pl.ds(0, mate_rows + sides * one_side)]).wait_send()
+
+    finish.append(parts_sent)
+    mid_s_here()
+    parts_received()
     for block in range(2 * ROWS + 1):
         offset = (row + block) * R1
         right = parts[pl.ds(offset, R1), :]
@@ -257,19 +336,18 @@
             right1 = right
     s1 = mid_s[own1, :]
 
-    def sweep1(field):
-        v = field[own1, :]
-        return v + s1 * (right1 - diag1[...] * v - level_apply(tiles1, field, cols1, base1, R1, 8))
-
-    mid_b[own1, :] = sweep1(mid_a)
-    send_middle(4, mid_b)
-    rest1[...] = right1 - diag1[...] * mid_b[own1, :]
+    v = mid_a[own1, :]
+    mid_b[own1, :] = v + s1 * (
+        right1 - diag1[...] * v - block_rows(all_products(tiles1, mid_a, cols1, base1), R1, 8)
+    )
+    mid_b_here = exchange_middle(4, mid_b)
+    rest1[...] = rest_of(right1, diag1, tiles1, mid_b, own1, R1, 8)
     for copy in coarse:
         copy.wait()
     diagonals(tiles2, scale2, NB2, 8)
     scale2[...] = relax / (diag2[...] + scale2[...])
-    middle_wait(4, mid_b)
-    part2 = restrict(tiles1, mid_b, cols1, base1, rest1, interp1, owner1, R1, NB2, 8)
+    mid_b_here()
+    part2 = restrict(neighbour_products(tiles1, mid_b, cols1), rest1, interp1, owner1, R1, NB2, 8)
 
     line_slot = core * ROWS + row
     near[line_slot] = part2
@@ -289,34 +367,35 @@
 
     v2 = right2 * scale2[...]
     field2[...] = v2
-    v2 = v2 + scale2[...] * (right2 - diag2[...] * v2 - level_apply(tiles2, field2, cols2, 0, NB2, 16))
+    product2 = block_rows(all_products(tiles2, field2, cols2, 0), NB2, 16)
+    v2 = v2 + scale2[...] * (right2 - diag2[...] * v2 - product2)
     out2[...] = v2
 
+    def sweep1(field, here):
+        started = field[own1, :] + s1 * rest_of(right1, diag1, tiles1, field, own1, R1, 8)
+        here()
+        return started - s1 * block_rows(neighbour_products(tiles1, field, cols1), R1, 8)
+
     mid_c[own1, :] = mid_b[own1, :] + prolong(interp1, out2, owner1, R1, 8)
-    send_middle(7, mid_c)
-    middle_wait(7, mid_c)
-    mid_d[own1, :] = sweep1(mid_c)
-    send_middle(8, mid_d)
-    middle_wait(8, mid_d)
+    mid_c_here = exchange_middle(7, mid_c)
+    mid_d[own1, :] = sweep1(mid_c, mid_c_here)
+    mid_d_here = exchange_middle(8, mid_d)
     place1 = pl.ds(row * R1, R1)
-    out1[place1, :] = sweep1(mid_d)
+    out1[place1, :] = sweep1(mid_d, mid_d_here)
     for mate in mates:
         send(9, out1.at[place1], out1.at[place1], mate)
     arrivals(9, out1.at[pl.ds(0, R0 - R1)]).wait_recv()
 
     fine_c[own0, :] = fine_b[own0, :] + prolong(interp0, out1, owner0, R0, 16)
-    send_fine(10, fine_c)
-    fine_wait(10, fine_c)
-    fine_d[own0, :] = sweep0(fine_c)
-    send_fine(11, fine_d)
-    fine_wait(11, fine_d)
-    out0[...] = sweep0(fine_d)
-
+    fine_c_here = exchange_fine(10, fine_c)
+    fine_d[own0, :] = sweep0(fine_c, fine_c_here)
+    fine_d_here = exchange_fine(11, fine_d)
+    out0[...] = sweep0(fine_d, fine_d_here)
+
+    for sent in finish:
+        sent()
     for index, like in (
-        (0, fine_a.at[pl.ds(0, 2 * R0)]), (1, mid_s.at[pl.ds(0, 2 * R0)]), (2, fine_b.at[pl.ds(0, 2 * R0)]),
-        (3, parts.at[pl.ds(0, 8 * R0)]), (4, mid_b.at[pl.ds(0, 2 * R0)]), (5, near.at[pl.ds(0, 2 * ROWS - 1)]),
-        (6, far.at[pl.ds(0, planes - 1)]), (7, mid_c.at[pl.ds(0, 2 * R0)]), (8, mid_d.at[pl.ds(0, 2 * R0)]),
-        (9, out1.at[pl.ds(0, R0 - R1)]), (10, fine_c.at[pl.ds(0, 2 * R0)]), (11, fine_d.at[pl.ds(0, 2 * R0)]),
+        (5, near.at[pl.ds(0, 2 * ROWS - 1)]), (6, far.at[pl.ds(0, planes - 1)]), (9, out1.at[pl.ds(0, R0 - R1)]),
     ):
         arrivals(index, like).wait_send()
 
@@ -347,8 +426,8 @@
     out_shape = tuple(jax.ShapeDtypeStruct((n, TILE), f32) for n in (R0, R0, NB2))
     results = pl.pallas_call(
         functools.partial(kernel, groups),
-        out_shape=out_shape,
-        in_specs=[pl.BlockSpec(memory_space=pl.ANY)] * len(arguments),
+        out_shape=tuple(vmem(n, TILE) for n in (R0, R0, NB2)),
+        in_specs=[pl.BlockSpec(memory_space=pltpu.HBM)] * len(arguments),
         out_specs=(pl.BlockSpec(memory_space=pltpu.VMEM),) * 3,
         scratch_shapes=scratch,
         compiler_params=pltpu.CompilerParams(
@@ -359,9 +438,10 @@
     return pl.pallas_call(
         hand_over,
         out_shape=out_shape,
-        in_specs=[pl.BlockSpec(memory_space=pltpu.HBM)] * 3,
+        in_specs=[pl.BlockSpec(memory_space=pl.ANY)] * 3,
         out_specs=(pl.BlockSpec(memory_space=pltpu.HBM),) * 3,
         scratch_shapes=[pltpu.SemaphoreType.DMA((3,))],
+        compiler_params=pltpu.CompilerParams(vmem_limit_bytes=2**20),
         name="results",
     )(*results)
 

time: 69.5 us -> 61.1 us (0.88)
  the two profiles are of different devices: /device:TPU:0 before, /device:TPU:8 now
where the time goes in v3:
time: 61.1 us; the launch traced here: 61 us
  Pallas kernels  60.3 us (99%)
  between operations  0.64 us (1%)
    pallas_call x1, Pallas kernels, shards(): pl.pallas_call(functools.partial(kernel, groups), out_shape=tuple((vmem(n...  59.7 us

profile of v3, /device:TPU:8, one launch (start us, length us, event | category | flops | bytes accessed | tf_op | source)
XLA Modules:
  0.0 61.0 jit_solution(2417704882398880539)
XLA Ops:
  0.6 59.7 %vcycle.1 = (f32[32,128]{1,0:T(8,128)S(1)}, f32[32,128]{1,0:T(8,128)S(1)}, f32[16,128]{1,0:T(8,128)S(1)}) custom-call(f32[32,128]{1,0:T(8,128)} %rhs_hbm.1, f32[32,5,128,128]{3,2,1,0:T(8,128)} %tiles0_hbm.1, f32[32,128]{1,0:T(8,128)} %diag0_hbm.1, s32[4,32]{1,0:T(4,128)} %bitcast.3, f32[8,5,128,128]{3,2,1,0:T(8,128)} %tiles1_hbm.1, f32[8,128]{1,0:T(8,128)} %diag1_hbm.1, ...), custom_call_target="tpu_custom_call" | custom-call | tf_op jit(solution)/shard_map/vcycle/pallas_call | solution.py:427
  60.4 0.6 %results.1 = (f32[32,128]{1,0:T(8,128)}, f32[32,128]{1,0:T(8,128)}, f32[16,128]{1,0:T(8,128)}) custom-call(f32[32,128]{1,0:T(8,128)S(1)} %get-tuple-element.6.refs_0_, f32[32,128]{1,0:T(8,128)S(1)} %get-tuple-element.7.refs_1_, f32[16,128]{1,0:T(8,128)S(1)} %get-tuple-element.8.refs_2_), custom_call_target="tpu_custom_call" | custom-call | tf_op jit(solution)/shard_map/results/pallas_call | solution.py:438

commit v4 on v3

--- a/solution.py
+++ b/solution.py
@@ -28,7 +28,7 @@
     return lax.div(place, ROWS), lax.rem(place, ROWS)
 
 
-STEPS = (4, -4, 3, -3, 2, -2, 1, -1)
+STEPS = (2, -2, 1, -1, 3, -3, 4, -4)
 
 
 def plane_peers(group, row, planes):
@@ -94,17 +94,23 @@
     return block_rows(lambda b: interp[b] * coarse[pl.ds(owner[b] & last, 1), :], count, unroll)
 
 
-def restrict(products_of, rest, interp, owner, count, targets, unroll):
+def restrict(residual_of, interp, owner, count, targets, unroll):
+    place = lax.broadcasted_iota(jnp.int32, (targets, TILE), 0)
+
+    def step(b, sums):
+        lifted = jnp.sum(interp[b] * residual_of(b), axis=0, keepdims=True)
+        return sums + jnp.where(place == owner[b] & (targets - 1), lifted, 0.0)
+
+    return lax.fori_loop(0, count, step, jnp.zeros((targets, TILE), jnp.float32), unroll=unroll)
+
+
+def as_columns(rows):
     eye = eye_mask()
-    place = lax.broadcasted_iota(jnp.int32, (targets, TILE), 0)
-
-    def step(b, sums):
-        products = products_of(b)
-        residual = lane_sums(jnp.where(eye, rest[pl.ds(b, 1), :], 0.0) - products)
-        lifted = jnp.sum(interp[b] * residual, axis=0, keepdims=True)
-        return sums + jnp.where(place == owner[b] & (targets - 1), lifted, 0.0)
-
-    return lax.fori_loop(0, count, step, jnp.zeros((targets, TILE), jnp.float32), unroll=unroll)
+    return lambda b: lane_sums(jnp.where(eye, rows[pl.ds(b, 1), :], 0.0))
+
+
+def summed(products):
+    return lambda b: lane_sums(products(b))
 
 
 def diagonals(tiles, out, count, unroll):
@@ -124,7 +130,7 @@
     out0, out1, out2,
     rhs, tiles0, diag0, cols0, tiles1, diag1, cols1,
     tiles2, diag2, cols2, interp0, owner0, interp1, owner1,
-    scale0, scale1, scale2, rest0, rest1, field2,
+    scale0, scale1, scale2, rest0, rest1, rest2, field2, picked2,
     fine_a, fine_b, fine_c, fine_d, mid_s, mid_a, mid_b, mid_c, mid_d,
     partial, parts, near, far,
     load_sem, send_sem, recv_sem,
@@ -168,9 +174,6 @@
         load(13, diag2_hbm, diag2),
         load(14, cols2_hbm, cols2),
     ]
-    for copy in first:
-        copy.start()
-
     mates = [(group, lax.rem(row + step, ROWS)) for step in range(1, ROWS)]
     far_peers = plane_peers(group, row, planes)
     after, before = lax.rem(group + 1, groups), lax.rem(group + groups - 1, groups)
@@ -190,6 +193,8 @@
     def _():
         greet([(before, place) for place in range(ROWS)])
 
+    for copy in first:
+        copy.start()
     greet(mates + far_peers)
     greeted = len(mates + far_peers) + jnp.where(has_after, ROWS, 0) + jnp.where(has_before, ROWS, 0)
 
@@ -263,7 +268,7 @@
     def sweep0(field, here):
         started = field[own0, :] + scale0[...] * rest_of(rhs[...], diag0, tiles0, field, own0, R0, 16)
         here()
-        return started - scale0[...] * block_rows(neighbour_products(tiles0, field, cols0), R0, 16)
+        return started - scale0[...] * block_rows(neighbour_products(tiles0, field, cols0), R0, 32)
 
     for copy in fine:
         copy.wait()
@@ -271,14 +276,15 @@
         copy.start()
     fine_b[own0, :] = sweep0(fine_a, fine_a_here)
     fine_b_here = exchange_fine(2, fine_b)
-    rest0[...] = rest_of(rhs[...], diag0, tiles0, fine_b, own0, R0, 16)
     for copy in middle:
         copy.wait()
     diagonals(tiles1, scale1, R1, 8)
     mid_s[own1, :] = relax / (diag1[...] + scale1[...])
     mid_s_here = exchange_middle(1, mid_s)
+    rest0[...] = rest_of(rhs[...], diag0, tiles0, fine_b, own0, R0, 16)
+    part = restrict(as_columns(rest0), interp0, owner0, R0, R0, 8)
     fine_b_here()
-    part = restrict(neighbour_products(tiles0, fine_b, cols0), rest0, interp0, owner0, R0, R0, 8)
+    part = part - restrict(summed(neighbour_products(tiles0, fine_b, cols0)), interp0, owner0, R0, R0, 16)
 
     partial[...] = part
     slot = row * (3 * R0)
@@ -341,16 +347,18 @@
         right1 - diag1[...] * v - block_rows(all_products(tiles1, mid_a, cols1, base1), R1, 8)
     )
     mid_b_here = exchange_middle(4, mid_b)
-    rest1[...] = rest_of(right1, diag1, tiles1, mid_b, own1, R1, 8)
     for copy in coarse:
         copy.wait()
+    rest1[...] = rest_of(right1, diag1, tiles1, mid_b, own1, R1, 8)
+    part2 = restrict(as_columns(rest1), interp1, owner1, R1, NB2, 8)
     diagonals(tiles2, scale2, NB2, 8)
     scale2[...] = relax / (diag2[...] + scale2[...])
     mid_b_here()
-    part2 = restrict(neighbour_products(tiles1, mid_b, cols1), rest1, interp1, owner1, R1, NB2, 8)
 
     line_slot = core * ROWS + row
-    near[line_slot] = part2
+    near[line_slot] = part2 - restrict(
+        summed(neighbour_products(tiles1, mid_b, cols1)), interp1, owner1, R1, NB2, 8
+    )
     for peer in chip_line_peers(group, row):
         send(5, near.at[line_slot], near.at[line_slot], peer)
     arrivals(5, near.at[pl.ds(0, 2 * ROWS - 1)]).wait_recv()
@@ -367,17 +375,27 @@
 
     v2 = right2 * scale2[...]
     field2[...] = v2
-    product2 = block_rows(all_products(tiles2, field2, cols2, 0), NB2, 16)
-    v2 = v2 + scale2[...] * (right2 - diag2[...] * v2 - product2)
-    out2[...] = v2
+    rest2[...] = v2 + scale2[...] * (right2 - diag2[...] * v2)
+
+    def coarse_products(b):
+        return all_products(tiles2, field2, cols2, 0)(b)
+
+    def owned(b):
+        return owner1[b] & (NB2 - 1)
+
+    product2 = block_rows(lambda b: coarse_products(owned(b)), R1, 8)
+    for b in range(R1):
+        here = pl.ds(owned(b), 1)
+        picked2[pl.ds(b, 1), :] = rest2[here, :] - scale2[here, :] * product2[b:b + 1]
+    mid_c[own1, :] = mid_b[own1, :] + block_rows(lambda b: interp1[b] * picked2[pl.ds(b, 1), :], R1, 8)
+    mid_c_here = exchange_middle(7, mid_c)
+    out2[...] = rest2[...] - scale2[...] * block_rows(coarse_products, NB2, 16)
 
     def sweep1(field, here):
         started = field[own1, :] + s1 * rest_of(right1, diag1, tiles1, field, own1, R1, 8)
         here()
         return started - s1 * block_rows(neighbour_products(tiles1, field, cols1), R1, 8)
 
-    mid_c[own1, :] = mid_b[own1, :] + prolong(interp1, out2, owner1, R1, 8)
-    mid_c_here = exchange_middle(7, mid_c)
     mid_d[own1, :] = sweep1(mid_c, mid_c_here)
     mid_d_here = exchange_middle(8, mid_d)
     place1 = pl.ds(row * R1, R1)
@@ -419,8 +437,10 @@
         copies.append(space(argument.shape, argument.dtype))
     scratch = copies + [
         vmem(R0, TILE), vmem(R1, TILE), vmem(NB2, TILE), vmem(R0, TILE), vmem(R1, TILE), vmem(NB2, TILE),
+        vmem(NB2, TILE), vmem(R1, TILE),
         *(vmem(RING, TILE) for _ in range(9)),
-        vmem(R0, TILE), vmem(ROWS * 3 * R0, TILE), vmem(2 * ROWS, NB2, TILE), vmem(groups // 2, NB2, TILE),
+        vmem(R0, TILE), vmem(ROWS * 3 * R0, TILE),
+        vmem(2 * ROWS, NB2, TILE), vmem(groups // 2, NB2, TILE),
         pltpu.SemaphoreType.DMA((16,)), pltpu.SemaphoreType.DMA((12,)), pltpu.SemaphoreType.DMA((12,)),
     ]
     out_shape = tuple(jax.ShapeDtypeStruct((n, TILE), f32) for n in (R0, R0, NB2))

time: 61.1 us -> 60.3 us (0.987)
  Pallas kernels: 60.3 us -> 59.5 us
    pallas_call x1, Pallas kernels: 59.7 us -> 58.9 us  [shards(): pl.pallas_call(functools.partial(kernel, groups), out_shape=tuple((vmem(n...]
where the time goes in v4:
time: 60.3 us; the launch traced here: 60.2 us
  Pallas kernels  59.5 us (99%)
  between operations  0.64 us (1%)
    pallas_call x1, Pallas kernels, shards(): pl.pallas_call(functools.partial(kernel, groups), out_shape=tuple((vmem(n...  58.9 us

profile of v4, /device:TPU:8, one launch (start us, length us, event | category | flops | bytes accessed | tf_op | source)
XLA Modules:
  0.0 60.2 jit_solution(5883134496144929858)
XLA Ops:
  0.6 58.9 %vcycle.1 = (f32[32,128]{1,0:T(8,128)S(1)}, f32[32,128]{1,0:T(8,128)S(1)}, f32[16,128]{1,0:T(8,128)S(1)}) custom-call(f32[32,128]{1,0:T(8,128)} %rhs_hbm.1, f32[32,5,128,128]{3,2,1,0:T(8,128)} %tiles0_hbm.1, f32[32,128]{1,0:T(8,128)} %diag0_hbm.1, s32[4,32]{1,0:T(4,128)} %bitcast.3, f32[8,5,128,128]{3,2,1,0:T(8,128)} %tiles1_hbm.1, f32[8,128]{1,0:T(8,128)} %diag1_hbm.1, ...), custom_call_target="tpu_custom_call" | custom-call | tf_op jit(solution)/shard_map/vcycle/pallas_call | solution.py:447
  59.5 0.6 %results.1 = (f32[32,128]{1,0:T(8,128)}, f32[32,128]{1,0:T(8,128)}, f32[16,128]{1,0:T(8,128)}) custom-call(f32[32,128]{1,0:T(8,128)S(1)} %get-tuple-element.6.refs_0_, f32[32,128]{1,0:T(8,128)S(1)} %get-tuple-element.7.refs_1_, f32[16,128]{1,0:T(8,128)S(1)} %get-tuple-element.8.refs_2_), custom_call_target="tpu_custom_call" | custom-call | tf_op jit(solution)/shard_map/results/pallas_call | solution.py:458

commit v5 on v4

--- a/solution.py
+++ b/solution.py
@@ -284,7 +284,7 @@
     rest0[...] = rest_of(rhs[...], diag0, tiles0, fine_b, own0, R0, 16)
     part = restrict(as_columns(rest0), interp0, owner0, R0, R0, 8)
     fine_b_here()
-    part = part - restrict(summed(neighbour_products(tiles0, fine_b, cols0)), interp0, owner0, R0, R0, 16)
+    part = part - restrict(summed(neighbour_products(tiles0, fine_b, cols0)), interp0, owner0, R0, R0, 32)
 
     partial[...] = part
     slot = row * (3 * R0)
@@ -404,7 +404,7 @@
         send(9, out1.at[place1], out1.at[place1], mate)
     arrivals(9, out1.at[pl.ds(0, R0 - R1)]).wait_recv()
 
-    fine_c[own0, :] = fine_b[own0, :] + prolong(interp0, out1, owner0, R0, 16)
+    fine_c[own0, :] = fine_b[own0, :] + prolong(interp0, out1, owner0, R0, 32)
     fine_c_here = exchange_fine(10, fine_c)
     fine_d[own0, :] = sweep0(fine_c, fine_c_here)
     fine_d_here = exchange_fine(11, fine_d)

time: 60.3 us -> 60.1 us (level)
  no operation moved by 1% of the time
where the time goes in v5:
time: 60.1 us; the launch traced here: 59.9 us
  Pallas kernels  59.3 us (99%)
  between operations  0.64 us (1%)
    pallas_call x1, Pallas kernels, shards(): pl.pallas_call(functools.partial(kernel, groups), out_shape=tuple((vmem(n...  58.7 us

profile of v5, /device:TPU:8, one launch (start us, length us, event | category | flops | bytes accessed | tf_op | source)
XLA Modules:
  0.0 59.9 jit_solution(7243496797977760894)
XLA Ops:
  0.6 58.7 %vcycle.1 = (f32[32,128]{1,0:T(8,128)S(1)}, f32[32,128]{1,0:T(8,128)S(1)}, f32[16,128]{1,0:T(8,128)S(1)}) custom-call(f32[32,128]{1,0:T(8,128)} %rhs_hbm.1, f32[32,5,128,128]{3,2,1,0:T(8,128)} %tiles0_hbm.1, f32[32,128]{1,0:T(8,128)} %diag0_hbm.1, s32[4,32]{1,0:T(4,128)} %bitcast.3, f32[8,5,128,128]{3,2,1,0:T(8,128)} %tiles1_hbm.1, f32[8,128]{1,0:T(8,128)} %diag1_hbm.1, ...), custom_call_target="tpu_custom_call" | custom-call | tf_op jit(solution)/shard_map/vcycle/pallas_call | solution.py:447
  59.3 0.6 %results.1 = (f32[32,128]{1,0:T(8,128)}, f32[32,128]{1,0:T(8,128)}, f32[16,128]{1,0:T(8,128)}) custom-call(f32[32,128]{1,0:T(8,128)S(1)} %get-tuple-element.6.refs_0_, f32[32,128]{1,0:T(8,128)S(1)} %get-tuple-element.7.refs_1_, f32[16,128]{1,0:T(8,128)S(1)} %get-tuple-element.8.refs_2_), custom_call_target="tpu_custom_call" | custom-call | tf_op jit(solution)/shard_map/results/pallas_call | solution.py:458
